TPU v7x, 32 devices: a whole 2x2x4 slice. The times are simulated.
32 devices in a mesh: groups: 2 (over y), cls: 4 (over x, core), proj: 4 (over z).
Axes of the slice: x: 2, y: 2, z: 4, core: 2. Of those that a mesh axis runs over, the one named last changes fastest.
Arguments:
- particles: bfloat16 [512, 4096], P(('groups', 'cls', 'proj')), parts along dimension 0, may hold values from -6 to 6
- classes: int32 [512, 1], P(('groups', 'cls', 'proj')), parts along dimension 0, may hold values from 0 to 3; in each aligned block of 16 rows (0 to 15, 16 to 31, ...) at most 12 rows name the same one
- windows: int32 [512, 2], P(('groups', 'cls', 'proj')), parts along dimension 0, may hold values from -3 to 3
- pose_lists: int32 [512, 8], P(('groups', 'cls', 'proj')), parts along dimension 0, may hold values from 0 to 15, all different within a row
- inverse_noise: bfloat16 [512], P(('groups', 'cls', 'proj')), parts along dimension 0, may hold values from 0.19921875 to 2
- projections: bfloat16 [4, 2048, 4096], P('cls', 'proj'), may hold values from -0.09375 to 0.09375
Outputs:
- posterior: float32 [512, 16, 2048], P(('groups', 'cls', 'proj')), parts along dimension 0
- evidence: float32 [512], P(('groups', 'cls', 'proj')), parts along dimension 0
There are 2 independent parts, one for each index of `groups`. A program takes and returns all parts, laid end to end along the dimension named above; an argument that names none is the same for every part. Nothing has to cross between parts.
Inputs may be any that keep to these rules, and one draw needn't show every extreme that they name: `classes`: within the rows of one device (aligned blocks of 16 rows) no class group is named by more than 12 rows, and in every draw some class group is named by exactly 12 rows of some device. `pose_lists`: each row names 8 different pose blocks.
All inputs are finite; a program needn't handle non-finite values.
Results may differ from a plain program's by a relative error of at most 0.0069.
Values may be sent and summed in bfloat16 or wider, within the bound.
No kernel may reach another device: no remote copies, remote signals or barrier semaphores. Data moves between devices by JAX's collectives and lax.ppermute only.
A program may use at most 128 MiB of HBM per device.

v0:
```python
import functools
import math

import jax
import jax.numpy as jnp
from jax import lax
from jax.experimental import pallas as pl
from jax.experimental.pallas import tpu as pltpu
from jax.sharding import PartitionSpec as P

IMG = 64
KF = 2048
J = 2048
NB = 16
SW = 4
SH = 16
LANES = 128
WIDTH = 2 * KF + LANES
HALVES = 2 * KF // LANES
TILE = 8
TURN = 1024
GROUP = 4
BLOCK = J // NB
CHUNKS = 2
BF16_MAX = float(jnp.finfo(jnp.bfloat16).max)


def unit_circle(turn):
    turn = turn - IMG * jnp.floor(turn * (1.0 / IMG) + 0.5)
    half = turn * (math.pi / IMG)
    square = half * half
    sine, cosine = jnp.zeros_like(half), jnp.zeros_like(half)
    for n in (13, 11, 9, 7, 5, 3, 1):
        sine = sine * square + (-1.0) ** (n // 2) / math.factorial(n)
    for n in (14, 12, 10, 8, 6, 4, 2, 0):
        cosine = cosine * square + (-1.0) ** (n // 2) / math.factorial(n)
    sine = sine * half
    return 1.0 - 2.0 * sine * sine, 2.0 * sine * cosine


def pack_kernel(particles_ref, classes_ref, windows_ref, poses_ref, noise_ref, *refs):
    outs, facts = refs[:-1], refs[-1]
    count = particles_ref.shape[0]
    held = NB + 4 + 4
    line = lax.broadcasted_iota(jnp.int32, (held, count), 0)

    def spread(row):
        return jnp.broadcast_to(row, (held, count))

    column = jnp.where(line == 0, spread(classes_ref[...]).astype(jnp.float32), 0.0)
    column = jnp.where(line == 1, spread(windows_ref[0:1, :]).astype(jnp.float32), column)
    column = jnp.where(line == 2, spread(windows_ref[1:2, :]).astype(jnp.float32), column)
    column = jnp.where(line == 3, spread(noise_ref[...].astype(jnp.float32)), column)
    for n in range(poses_ref.shape[0]):
        column = jnp.where(line == spread(poses_ref[n:n + 1, :]) + 4, 1.0, column)
    facts[...] = jnp.zeros(facts.shape, jnp.float32)
    facts[0:held, 0:count] = column
    tail = facts[...].T[0:count, :].astype(jnp.bfloat16)
    part = count // len(outs)
    for j, out_ref in enumerate(outs):
        out_ref[:, 0:2 * KF] = particles_ref[j * part:(j + 1) * part, :]
        out_ref[:, 2 * KF:] = tail[j * part:(j + 1) * part, :]


def pack(particles, classes, windows, pose_lists, inverse_noise):
    count = particles.shape[0]
    whole = pl.BlockSpec(memory_space=pltpu.VMEM)
    return pl.pallas_call(
        pack_kernel,
        out_shape=[jax.ShapeDtypeStruct((count // CHUNKS, WIDTH), jnp.bfloat16)] * CHUNKS,
        in_specs=[whole] * 5,
        out_specs=[whole] * CHUNKS,
        scratch_shapes=[pltpu.VMEM((LANES, LANES), jnp.float32)],
        name="pack",
    )(particles, classes.T, windows.T, pose_lists.T, inverse_noise[None, :])


def turn_kernel(own_ref, other_ref, own_out, other_out, cos_ref, sin_ref):
    own_out[...] = own_ref[...].T
    other_out[...] = other_ref[...].T

    @pl.when(pl.program_id(0) == 0)
    def _():
        shift = lax.broadcasted_iota(jnp.int32, cos_ref.shape, 0)
        c = lax.broadcasted_iota(jnp.int32, cos_ref.shape, 1)
        kx, ky = c % IMG - IMG // 2, c // IMG
        turn = (shift % SW - SW // 2) * kx + (shift // SW - SW // 2) * ky
        cos_ref[...], sin_ref[...] = unit_circle(turn.astype(jnp.float32))


def turn(own_panel, other_panel):
    depth, width = own_panel.shape
    turned = jax.ShapeDtypeStruct((width, depth), own_panel.dtype)
    table = jax.ShapeDtypeStruct((SH, KF), jnp.float32)
    fixed = pl.BlockSpec((SH, KF), lambda i: (0, 0))
    return pl.pallas_call(
        turn_kernel,
        grid=(width // TURN,),
        out_shape=[turned, turned, table, table],
        in_specs=[pl.BlockSpec((depth, TURN), lambda i: (0, i))] * 2,
        out_specs=[pl.BlockSpec((TURN, depth), lambda i: (i, 0))] * 2 + [fixed] * 2,
        compiler_params=pltpu.CompilerParams(vmem_limit_bytes=20 * 1024 * 1024),
        cost_estimate=pl.CostEstimate(flops=0, bytes_accessed=16 << 20, transcendentals=0),
        name="turn",
    )(own_panel, other_panel)


def score_kernel(
    me_ref, rows_ref, own_any, other_any, cos_ref, sin_ref, out_ref,
    centred, shifted, scores, details, facts, members, panels, fact_sem, panel_sems,
):
    pieces, count, _ = rows_ref.shape
    for s in range(pieces):
        details[s * count:(s + 1) * count, :] = rows_ref[s, :, 2 * KF:].astype(jnp.float32)
    send = pltpu.make_async_copy(details, facts, fact_sem)
    send.start()
    loads = [
        pltpu.make_async_copy(panel, panels.at[n], panel_sems.at[n])
        for n, panel in enumerate((own_any, other_any))
    ]
    for copy in loads:
        copy.start()

    lane = lax.broadcasted_iota(jnp.int32, (count, LANES), 1)
    kx = (lane % IMG - IMG // 2).astype(jnp.float32)
    odd = (lane // IMG).astype(jnp.float32)
    for s in range(pieces):
        fact = details[s * count:(s + 1) * count, :]
        wx = jnp.broadcast_to(fact[:, 1:2], (count, LANES))
        wy = jnp.broadcast_to(fact[:, 2:3], (count, LANES))
        cosine, sine = unit_circle(wx * kx + wy * odd)
        step_cos, step_sin = unit_circle(wy * 2.0)
        for t in range(KF // LANES):
            at = slice(t * LANES, (t + 1) * LANES)
            to = slice(KF + t * LANES, KF + (t + 1) * LANES)
            re = rows_ref[s, :, at].astype(jnp.float32)
            im = rows_ref[s, :, to].astype(jnp.float32)
            centred[pl.ds(s * count * HALVES + t, count, HALVES), :] = re * cosine + im * sine
            centred[pl.ds(s * count * HALVES + HALVES // 2 + t, count, HALVES), :] = im * cosine - re * sine
            cosine, sine = (
                cosine * step_cos - sine * step_sin,
                sine * step_cos + cosine * step_sin,
            )
    send.wait()

    own = me_ref[0].astype(jnp.float32)
    other = (me_ref[0] ^ 1).astype(jnp.float32)
    first_block = me_ref[1]

    def sort_row(row, filled):
        label = facts[row, 0]
        members[0, filled[0]] = row
        members[1, filled[1]] = row
        return (
            filled[0] + (label == own).astype(jnp.int32),
            filled[1] + (label == other).astype(jnp.int32),
        )

    totals = lax.fori_loop(0, pieces * count, sort_row, (jnp.int32(0), jnp.int32(0)), unroll=8)

    for which, copy in enumerate(loads):
        copy.wait()

        @pl.loop(0, (totals[which] + TILE - 1) // TILE)
        def _(tile):
            base = tile * TILE
            present = jnp.minimum(totals[which] - base, TILE)

            spots = []
            for q in range(TILE):
                row = jnp.where(q < present, members[which, base + q], 0)
                spots.append(pl.multiple_of(row * HALVES, HALVES))
            for t in range(KF // LANES):
                at = slice(t * LANES, (t + 1) * LANES)
                to = slice(KF + t * LANES, KF + (t + 1) * LANES)
                cosine, sine = cos_ref[:, at], sin_ref[:, at]
                for q in range(TILE):
                    place = slice(q * SH, (q + 1) * SH)
                    base_re = spots[q] + t // 8 * 8
                    re = centred[pl.ds(pl.multiple_of(base_re, 8), 8), :][t % 8:t % 8 + 1, :]
                    im = centred[pl.ds(pl.multiple_of(base_re + HALVES // 2, 8), 8), :][t % 8:t % 8 + 1, :]
                    re = jnp.broadcast_to(re, (SH, LANES))
                    im = jnp.broadcast_to(im, (SH, LANES))
                    shifted[place, at] = (re * cosine + im * sine).astype(jnp.bfloat16)
                    shifted[place, to] = (im * cosine - re * sine).astype(jnp.bfloat16)

            scores[...] = jnp.dot(shifted[...], panels[which], preferred_element_type=jnp.float32)

            @pl.loop(0, present)
            def _(q):
                row = members[which, base + q]
                noise = facts[row, 3]
                place = pl.ds(pl.multiple_of(q * SH, SH), SH)
                for b in range(out_ref.shape[3] // BLOCK):
                    at = slice(b * BLOCK, (b + 1) * BLOCK)
                    allowed = facts[row, 4 + first_block + b]
                    term = jnp.minimum(jnp.exp(scores[place, at] * noise), BF16_MAX)
                    out_ref[row // count, row % count, :, at] = (term * allowed).astype(jnp.bfloat16)


def score(me, rows, own_panel, other_panel, cosine, sine):
    pieces, count, _ = rows.shape
    depth = own_panel.shape[1]
    total = pieces * count
    return pl.pallas_call(
        score_kernel,
        out_shape=jax.ShapeDtypeStruct((pieces, count, SH, depth), jnp.bfloat16),
        in_specs=[
            pl.BlockSpec(memory_space=pltpu.SMEM),
            pl.BlockSpec(memory_space=pltpu.VMEM),
            pl.BlockSpec(memory_space=pl.ANY),
            pl.BlockSpec(memory_space=pl.ANY),
            pl.BlockSpec(memory_space=pltpu.VMEM),
            pl.BlockSpec(memory_space=pltpu.VMEM),
        ],
        out_specs=pl.BlockSpec(memory_space=pltpu.VMEM),
        scratch_shapes=[
            pltpu.VMEM((total * HALVES, LANES), jnp.float32),
            pltpu.VMEM((TILE * SH, 2 * KF), jnp.bfloat16),
            pltpu.VMEM((TILE * SH, depth), jnp.float32),
            pltpu.VMEM((total, LANES), jnp.float32),
            pltpu.SMEM((total, LANES), jnp.float32),
            pltpu.SMEM((2, total + TILE), jnp.int32),
            pltpu.VMEM((2, 2 * KF, depth), jnp.bfloat16),
            pltpu.SemaphoreType.DMA,
            pltpu.SemaphoreType.DMA((2,)),
        ],
        compiler_params=pltpu.CompilerParams(vmem_limit_bytes=24 * 1024 * 1024),
        cost_estimate=pl.CostEstimate(
            flops=total * SH * depth * 4 * KF, bytes_accessed=16 << 20, transcendentals=0
        ),
        name="score",
    )(me, rows, own_panel, other_panel, cosine, sine)


def weigh_kernel(places, first, me_ref, *refs):
    parts, (weights_ref, log_ref) = refs[:places], refs[-2:]
    group, _, depth = parts[0].shape
    step = pl.program_id(0)

    @pl.when(step == 0)
    def _():
        log_ref[...] = refs[places + 1][...] if first else jnp.zeros(log_ref.shape, jnp.float32)

    lane = lax.broadcasted_iota(jnp.int32, log_ref.shape, 1)
    logs = log_ref[...]
    for g in range(group):
        total = sum(part[g].astype(jnp.float32) for part in parts)
        mean = jnp.sum(total, keepdims=True) / (SH * J)
        scale = 1.0 / mean
        for s in range(places):
            at = pl.multiple_of((me_ref[2] ^ s) * depth, depth)
            weights_ref[g, :, pl.ds(at, depth)] = parts[s][g].astype(jnp.float32) * scale
        logs = jnp.where(lane == first + step * group + g, jnp.log(mean), logs)
    log_ref[...] = logs


def weigh(me, parts, first, rows, before):
    places = len(parts)
    count, _, depth = parts[0].shape
    group = min(GROUP, count)
    logs = pl.BlockSpec((1, rows), lambda i: (0, 0))
    return pl.pallas_call(
        functools.partial(weigh_kernel, places, first),
        grid=(count // group,),
        out_shape=(
            jax.ShapeDtypeStruct((rows, SH, J), jnp.float32),
            jax.ShapeDtypeStruct((1, rows), jnp.float32),
        ),
        in_specs=[pl.BlockSpec(memory_space=pltpu.SMEM)]
        + [pl.BlockSpec((group, SH, depth), lambda i: (i, 0, 0))] * places
        + [pl.BlockSpec(memory_space=pl.ANY), logs][:len(before)],
        out_specs=(pl.BlockSpec((group, SH, J), lambda i: (first // group + i, 0, 0)), logs),
        input_output_aliases={places + 1: 0} if before else {},
        compiler_params=pltpu.CompilerParams(vmem_limit_bytes=16 * 1024 * 1024),
        name="weigh",
    )(me, *parts, *before)


def per_device(particles, classes, windows, pose_lists, inverse_noise, projections):
    owners = lax.axis_size("cls")
    places = lax.axis_size("proj")
    pairs = owners // 2
    label, place = lax.axis_index("cls"), lax.axis_index("proj")
    own_x = label // 2
    depth = projections.shape[1]
    me = jnp.stack([label, place * (depth // BLOCK), place]).astype(jnp.int32)

    def along_x(value, by):
        return lax.ppermute(value, "cls", [(i, i ^ (2 * by)) for i in range(owners)])

    def along_z(value, by):
        return lax.ppermute(value, "proj", [(i, i ^ by) for i in range(places)])

    chunks = pack(particles, classes, windows, pose_lists, inverse_noise)
    pieces = [[mine] + [along_z(mine, s) for s in range(1, places)] for mine in chunks]
    other_panel = lax.ppermute(projections[0], "cls", [(i, i ^ 1) for i in range(owners)])
    panels = turn(projections[0], other_panel)
    panels, pieces[1] = lax.optimization_barrier((panels, pieces[1]))
    columns = [jnp.stack(piece) for piece in pieces]
    far = [[along_x(column, f) for f in range(1, pairs)] for column in columns]
    far[0], columns[1:] = lax.optimization_barrier((far[0], columns[1:]))
    far_terms = []
    for group in far:
        terms = [score(me, rows, *panels) for rows in group]
        far_terms.append([along_x(t, f + 1) for f, t in enumerate(terms)])
    done, parts = (), None
    for j, column in enumerate(columns):
        column, terms = lax.optimization_barrier((column, terms))
        merged = score(me, column, *panels)
        owner_x = column[:, :, 2 * KF].astype(jnp.int32) // 2
        if j:
            far_terms[j], parts[1] = lax.optimization_barrier((far_terms[j], parts[1]))
            done = weigh(me, parts, (j - 1) * column.shape[1], particles.shape[0], done)
        for f in range(1, pairs):
            there = owner_x == (own_x ^ f)
            merged = jnp.where(there[:, :, None, None], far_terms[j][f - 1], merged)
        terms = merged
        parts = [merged[0]] + [along_z(merged[s], s) for s in range(1, places)]
    done = weigh(me, parts, (CHUNKS - 1) * column.shape[1], particles.shape[0], done)
    return done[0], done[1].reshape(-1)


def solution(mesh):
    placed = (
        P(("groups", "cls", "proj"), None),
        P(("groups", "cls", "proj"), None),
        P(("groups", "cls", "proj"), None),
        P(("groups", "cls", "proj"), None),
        P(("groups", "cls", "proj")),
        P("cls", "proj", None),
    )
    return jax.shard_map(
        per_device,
        mesh=mesh,
        in_specs=placed,
        out_specs=(P(("groups", "cls", "proj"), None, None), P(("groups", "cls", "proj"))),
        check_vma=False,
    )
```

profile of v0, /device:TPU:0, one launch (start us, length us, event | category | flops | bytes accessed | tf_op | source)
XLA Modules:
  0.0 68.3 jit_solution(2819618043368619830)
XLA Ops:
  0.6 0.5 collective-permute-start.4
  1.1 1.7 %pack.1 = (bf16[8,4224]{1,0:T(8,128)(2,1)}, bf16[8,4224]{1,0:T(8,128)(2,1)}) custom-call(bf16[16,4096]{1,0:T(8,128)(2,1)} %particles_ref.1, s32[1,16]{1,0:T(1,128)} %bitcast.45, s32[2,16]{1,0:T(2,128)} %bitcast.44, s32[8,16]{1,0:T(8,128)} %bitcast.43, bf16[1,16]{1,0:T(2,128)(2,1)} %bitcast.46), custom_call_target="tpu_custom_call" | custom-call | tf_op jit(solution)/shard_map/pack/pallas_call | solution.py:68
  2.8 4.6 %collective-permute-start.2 = (bf16[8,4224]{1,0:T(8,128)(2,1)}, bf16[8,4224]{1,0:T(8,128)(2,1)S(1)}, u32[]{:S(2)}, u32[]{:S(2)}) collective-permute-start(bf16[8,4224]{1,0:T(8,128)(2,1)} %get-tuple-element.26), channel_id=1, source_target_pairs={{0,3},{1,2},{2,1},{3,0},{4,7},{5,6},{6,5},{7,4},{8,11},{9,10},{10,... | collective-permute-start | bytes 202760 | tf_op jit(solution)/shard_map/ppermute | solution.py:293
  7.4 0.0 collective-permute-start
  7.4 0.6 collective-permute-start.1
  8.0 1.5 %collective-permute-start.5 = (bf16[8,4224]{1,0:T(8,128)(2,1)}, bf16[8,4224]{1,0:T(8,128)(2,1)S(1)}, u32[]{:S(2)}, u32[]{:S(2)}) collective-permute-start(bf16[8,4224]{1,0:T(8,128)(2,1)} %get-tuple-element.32), channel_id=1, source_target_pairs={{0,1},{1,0},{2,3},{3,2},{4,5},{5,4},{6,7},{7,6},{8,9},{9,8},{10,11... | collective-permute-start | bytes 202760 | tf_op jit(solution)/shard_map/ppermute | solution.py:293
  9.5 1.2 %collective-permute-done.2 = bf16[8,4224]{1,0:T(8,128)(2,1)S(1)} collective-permute-done((bf16[8,4224]{1,0:T(8,128)(2,1)}, bf16[8,4224]{1,0:T(8,128)(2,1)S(1)}, u32[]{:S(2)}, u32[]{:S(2)}) %collective-permute-start.2) | collective-permute-done | bytes 67616 | tf_op jit(solution)/shard_map/ppermute | solution.py:293
  10.7 1.7 %collective-permute-start.6 = (bf16[8,4224]{1,0:T(8,128)(2,1)}, bf16[8,4224]{1,0:T(8,128)(2,1)S(1)}, u32[]{:S(2)}, u32[]{:S(2)}) collective-permute-start(bf16[8,4224]{1,0:T(8,128)(2,1)} %get-tuple-element.32), channel_id=1, source_target_pairs={{0,2},{1,3},{2,0},{3,1},{4,6},{5,7},{6,4},{7,5},{8,10},{9,11},{10,... | collective-permute-start | bytes 202760 | tf_op jit(solution)/shard_map/ppermute | solution.py:293
  12.4 1.7 %collective-permute-done = bf16[8,4224]{1,0:T(8,128)(2,1)S(1)} collective-permute-done((bf16[8,4224]{1,0:T(8,128)(2,1)}, bf16[8,4224]{1,0:T(8,128)(2,1)S(1)}, u32[]{:S(2)}, u32[]{:S(2)}) %collective-permute-start) | collective-permute-done | bytes 67616 | tf_op jit(solution)/shard_map/ppermute | solution.py:293
  14.1 0.3 collective-permute-start.7
  14.4 0.0 collective-permute-done.1
  14.4 1.0 %pad_maximum_fusion.rows_ref = bf16[4,8,4224]{2,1,0:T(8,128)(2,1)S(1)} fusion(bf16[1,8,4224]{2,1,0:T(8,128)(2,1)S(1)} %bitcast.38, bf16[1,8,4224]{2,1,0:T(8,128)(2,1)S(1)} %bitcast.40, bf16[1,8,4224]{2,1,0:T(8,128)(2,1)S(1)} %bitcast.39, bf16[1,8,4224]{2,1,0:T(8,128)(2,1)} %bitcast.37), kind=kLoop, calls=%fused_computation.2 | loop fusion | flops 405504 | bytes 540672 | tf_op jit(solution)/shard_map/stack | solution.py:300
  15.4 1.6 %collective-permute-start.3 = (bf16[4,8,4224]{2,1,0:T(8,128)(2,1)S(1)}, bf16[4,8,4224]{2,1,0:T(8,128)(2,1)S(1)}, u32[]{:S(2)}, u32[]{:S(2)}) collective-permute-start(bf16[4,8,4224]{2,1,0:T(8,128)(2,1)S(1)} %pad_maximum_fusion.rows_ref), channel_id=1, source_target_pairs={{0,8},{4,12},{8,0},{12,4},{1,9},{5,13},{9,1},{13,5},{2,10},{6,14},... | collective-permute-start | bytes 811016 | tf_op jit(solution)/shard_map/ppermute | solution.py:290
  16.9 0.0 collective-permute-done.4.other_ref
  16.9 2.2 %copy-done = bf16[1,512,4096]{2,1,0:T(8,128)(2,1)S(1)} copy-done((bf16[1,512,4096]{2,1,0:T(8,128)(2,1)S(1)}, bf16[1,512,4096]{2,1,0:T(8,128)(2,1)}, u32[]{:S(2)}) %copy-start) | copy-done | bytes 4194328
  19.1 4.8 %turn.1 = (bf16[4096,512]{1,0:T(8,128)(2,1)S(1)}, bf16[4096,512]{1,0:T(8,128)(2,1)S(1)}, f32[16,2048]{1,0:T(8,128)S(1)}, f32[16,2048]{1,0:T(8,128)S(1)}) custom-call(bf16[512,4096]{1,0:T(8,128)(2,1)S(1)} %bitcast.34, bf16[512,4096]{1,0:T(8,128)(2,1)} %collective-permute-done.4.other_ref), custom_call_target="tpu_custom_call" | custom-call | bytes 16777216 | tf_op jit(solution)/shard_map/turn/pallas_call | solution.py:96
  23.9 0.0 collective-permute-done.5
  23.9 0.0 collective-permute-done.6
  23.9 0.0 collective-permute-done.7
  24.0 0.6 collective-permute-start.8
  24.6 0.1 pad_add_fusion.me_ref
  24.7 0.0 collective-permute-done.3.rows_ref
  24.7 5.7 %score.5 = bf16[4,8,16,512]{3,2,1,0:T(8,128)(2,1)S(1)} custom-call(s32[3]{0:T(128)S(1)} %pad_add_fusion.me_ref, bf16[4,8,4224]{2,1,0:T(8,128)(2,1)S(1)} %collective-permute-done.3.rows_ref, bf16[4096,512]{1,0:T(8,128)(2,1)S(1)} %get-tuple-element.37.own_any, bf16[4096,512]{1,0:T(8,128)(2,1)S(1)} %get-tuple-element.38.other_any, ...), custom_call_target="tpu_custom_call" | custom-call | flops 2147483648 | bytes 16777216 | tf_op jit(solution)/shard_map/score/pallas_call | solution.py:205
  30.4 0.1 collective-permute-start.9
  30.5 1.3 %collective-permute-done.8.rows_ref = bf16[4,8,4224]{2,1,0:T(8,128)(2,1)S(1)} collective-permute-done((bf16[4,8,4224]{2,1,0:T(8,128)(2,1)S(1)}, bf16[4,8,4224]{2,1,0:T(8,128)(2,1)S(1)}, u32[]{:S(2)}, u32[]{:S(2)}) %collective-permute-start.8) | collective-permute-done | bytes 270368 | tf_op jit(solution)/shard_map/ppermute | solution.py:290
  31.8 4.8 %score.4 = bf16[4,8,16,512]{3,2,1,0:T(8,128)(2,1)S(1)} custom-call(s32[3]{0:T(128)S(1)} %pad_add_fusion.me_ref, bf16[4,8,4224]{2,1,0:T(8,128)(2,1)S(1)} %collective-permute-done.8.rows_ref, bf16[4096,512]{1,0:T(8,128)(2,1)S(1)} %get-tuple-element.37.own_any, bf16[4096,512]{1,0:T(8,128)(2,1)S(1)} %get-tuple-element.38.other_any, ...), custom_call_target="tpu_custom_call" | custom-call | flops 2147483648 | bytes 16777216 | tf_op jit(solution)/shard_map/score/pallas_call | solution.py:205
  36.6 0.7 collective-permute-start.10
  37.2 0.1 convert_reduce_fusion.1
  37.4 4.8 %score.6 = bf16[4,8,16,512]{3,2,1,0:T(8,128)(2,1)S(1)} custom-call(s32[3]{0:T(128)S(1)} %pad_add_fusion.me_ref, bf16[4,8,4224]{2,1,0:T(8,128)(2,1)S(1)} %pad_maximum_fusion.rows_ref, bf16[4096,512]{1,0:T(8,128)(2,1)S(1)} %get-tuple-element.37.own_any, bf16[4096,512]{1,0:T(8,128)(2,1)S(1)} %get-tuple-element.38.other_any, ...), custom_call_target="tpu_custom_call" | custom-call | flops 2147483648 | bytes 16777216 | tf_op jit(solution)/shard_map/score/pallas_call | solution.py:205
  42.2 3.1 %collective-permute-done.9 = bf16[4,8,16,512]{3,2,1,0:T(8,128)(2,1)S(1)} collective-permute-done((bf16[4,8,16,512]{3,2,1,0:T(8,128)(2,1)S(1)}, bf16[4,8,16,512]{3,2,1,0:T(8,128)(2,1)S(1)}, u32[]{:S(2)}, u32[]{:S(2)}) %collective-permute-start.9) | collective-permute-done | bytes 524320 | tf_op jit(solution)/shard_map/ppermute | solution.py:290
  45.3 0.1 broadcast_select_fusion.1
  45.5 0.9 %collective-permute-start.11 = (bf16[8,16,512]{2,1,0:T(8,128)(2,1)S(1)}, bf16[8,16,512]{2,1,0:T(8,128)(2,1)S(1)}, u32[]{:S(2)}, u32[]{:S(2)}) collective-permute-start(bf16[8,16,512]{2,1,0:T(8,128)(2,1)S(1)} %get-tuple-element.53), channel_id=1, source_target_pairs={{0,1},{1,0},{2,3},{3,2},{4,5},{5,4},{6,7},{7,6},{8,9},{9,8},{10,11... | collective-permute-start | bytes 393224 | tf_op jit(solution)/shard_map/ppermute | solution.py:293
  46.4 3.2 %collective-permute-start.15 = (bf16[8,16,512]{2,1,0:T(8,128)(2,1)S(1)}, bf16[8,16,512]{2,1,0:T(8,128)(2,1)S(1)}, u32[]{:S(2)}, u32[]{:S(2)}) collective-permute-start(bf16[8,16,512]{2,1,0:T(8,128)(2,1)S(1)} %get-tuple-element.51), channel_id=1, source_target_pairs={{0,2},{1,3},{2,0},{3,1},{4,6},{5,7},{6,4},{7,5},{8,10},{9,11},{10,... | collective-permute-start | bytes 393224 | tf_op jit(solution)/shard_map/ppermute | solution.py:293
  49.6 0.3 collective-permute-start.16
  49.9 0.1 convert_reduce_fusion
  50.1 4.7 %score.7 = bf16[4,8,16,512]{3,2,1,0:T(8,128)(2,1)S(1)} custom-call(s32[3]{0:T(128)S(1)} %pad_add_fusion.me_ref, bf16[4,8,4224]{2,1,0:T(8,128)(2,1)S(1)} %pad_maximum_fusion.1.rows_ref, bf16[4096,512]{1,0:T(8,128)(2,1)S(1)} %get-tuple-element.37.own_any, bf16[4096,512]{1,0:T(8,128)(2,1)S(1)} %get-tuple-element.38.other_any, ...), custom_call_target="tpu_custom_call" | custom-call | flops 2147483648 | bytes 16777216 | tf_op jit(solution)/shard_map/score/pallas_call | solution.py:205
  54.8 0.0 collective-permute-done.11.refs_1_
  54.8 0.0 collective-permute-done.10
  54.8 0.1 broadcast_select_fusion
  55.0 0.3 collective-permute-start.12
  55.3 3.8 %collective-permute-start.13 = (bf16[8,16,512]{2,1,0:T(8,128)(2,1)S(1)}, bf16[8,16,512]{2,1,0:T(8,128)(2,1)S(1)}, u32[]{:S(2)}, u32[]{:S(2)}) collective-permute-start(bf16[8,16,512]{2,1,0:T(8,128)(2,1)S(1)} %get-tuple-element.55), channel_id=1, source_target_pairs={{0,2},{1,3},{2,0},{3,1},{4,6},{5,7},{6,4},{7,5},{8,10},{9,11},{10,... | collective-permute-start | bytes 393224 | tf_op jit(solution)/shard_map/ppermute | solution.py:293
  59.1 0.3 collective-permute-start.14
  59.4 0.0 collective-permute-done.15.refs_2_
  59.4 0.0 collective-permute-done.16.refs_3_
  59.4 1.8 %weigh.2 = (f32[16,16,2048]{2,1,0:T(8,128)}, f32[1,16]{1,0:T(1,128)S(1)}) custom-call(s32[3]{0:T(128)S(1)} %pad_add_fusion.me_ref, bf16[8,16,512]{2,1,0:T(8,128)(2,1)S(1)} %get-tuple-element.52.refs_0_, bf16[8,16,512]{2,1,0:T(8,128)(2,1)S(1)} %collective-permute-done.11.refs_1_, bf16[8,16,512]{2,1,0:T(8,128)(2,1)S(1)} %collective-permute-done.15.refs_2_, ...), custom_call_target="tpu_custom_call" | custom-call | tf_op jit(solution)/shard_map/weigh/pallas_call | solution.py:263
  61.2 1.1 %collective-permute-done.12.refs_1_ = bf16[8,16,512]{2,1,0:T(8,128)(2,1)S(1)} collective-permute-done((bf16[8,16,512]{2,1,0:T(8,128)(2,1)S(1)}, bf16[8,16,512]{2,1,0:T(8,128)(2,1)S(1)}, u32[]{:S(2)}, u32[]{:S(2)}) %collective-permute-start.12) | collective-permute-done | bytes 131104 | tf_op jit(solution)/shard_map/ppermute | solution.py:293
  62.3 4.3 %collective-permute-done.13.refs_2_ = bf16[8,16,512]{2,1,0:T(8,128)(2,1)S(1)} collective-permute-done((bf16[8,16,512]{2,1,0:T(8,128)(2,1)S(1)}, bf16[8,16,512]{2,1,0:T(8,128)(2,1)S(1)}, u32[]{:S(2)}, u32[]{:S(2)}) %collective-permute-start.13) | collective-permute-done | bytes 131104 | tf_op jit(solution)/shard_map/ppermute | solution.py:293
  66.6 1.7 %weigh.3 = (f32[16,16,2048]{2,1,0:T(8,128)}, f32[1,16]{1,0:T(1,128)}) custom-call(s32[3]{0:T(128)S(1)} %pad_add_fusion.me_ref, bf16[8,16,512]{2,1,0:T(8,128)(2,1)S(1)} %get-tuple-element.57.refs_0_, bf16[8,16,512]{2,1,0:T(8,128)(2,1)S(1)} %collective-permute-done.12.refs_1_, ...), custom_call_target="tpu_custom_call", output_to_operand_aliasing={{0}: (5, {})} | custom-call | tf_op jit(solution)/shard_map/weigh/pallas_call | solution.py:263
  (9 shorter events, 0.2 us)
Async XLA Ops:
  0.6 16.3 %collective-permute-start.4 = (bf16[512,4096]{1,0:T(8,128)(2,1)}, bf16[512,4096]{1,0:T(8,128)(2,1)}, u32[]{:S(2)}, u32[]{:S(2)}) collective-permute-start(bf16[512,4096]{1,0:T(8,128)(2,1)} %bitcast.33), channel_id=1, source_target_pairs={{0,4},{4,0},{8,12},{12,8},{1,5},{5,1},{9,13},{13,9},{2,6},{6,2},{1... | collective-permute-start | bytes 12582920 | tf_op jit(solution)/shard_map/ppermute | solution.py:297
  2.8 7.9 %collective-permute-start.2 = (bf16[8,4224]{1,0:T(8,128)(2,1)}, bf16[8,4224]{1,0:T(8,128)(2,1)S(1)}, u32[]{:S(2)}, u32[]{:S(2)}) collective-permute-start(bf16[8,4224]{1,0:T(8,128)(2,1)} %get-tuple-element.26), channel_id=1, source_target_pairs={{0,3},{1,2},{2,1},{3,0},{4,7},{5,6},{6,5},{7,4},{8,11},{9,10},{10,... | collective-permute-start | bytes 202760 | tf_op jit(solution)/shard_map/ppermute | solution.py:293
  7.4 6.6 %collective-permute-start = (bf16[8,4224]{1,0:T(8,128)(2,1)}, bf16[8,4224]{1,0:T(8,128)(2,1)S(1)}, u32[]{:S(2)}, u32[]{:S(2)}) collective-permute-start(bf16[8,4224]{1,0:T(8,128)(2,1)} %get-tuple-element.26), channel_id=1, source_target_pairs={{0,1},{1,0},{2,3},{3,2},{4,5},{5,4},{6,7},{7,6},{8,9},{9,8},{10,11... | collective-permute-start | bytes 202760 | tf_op jit(solution)/shard_map/ppermute | solution.py:293
  7.4 7.0 %collective-permute-start.1 = (bf16[8,4224]{1,0:T(8,128)(2,1)}, bf16[8,4224]{1,0:T(8,128)(2,1)S(1)}, u32[]{:S(2)}, u32[]{:S(2)}) collective-permute-start(bf16[8,4224]{1,0:T(8,128)(2,1)} %get-tuple-element.26), channel_id=1, source_target_pairs={{0,2},{1,3},{2,0},{3,1},{4,6},{5,7},{6,4},{7,5},{8,10},{9,11},{10,... | collective-permute-start | bytes 202760 | tf_op jit(solution)/shard_map/ppermute | solution.py:293
  8.0 15.9 %collective-permute-start.5 = (bf16[8,4224]{1,0:T(8,128)(2,1)}, bf16[8,4224]{1,0:T(8,128)(2,1)S(1)}, u32[]{:S(2)}, u32[]{:S(2)}) collective-permute-start(bf16[8,4224]{1,0:T(8,128)(2,1)} %get-tuple-element.32), channel_id=1, source_target_pairs={{0,1},{1,0},{2,3},{3,2},{4,5},{5,4},{6,7},{7,6},{8,9},{9,8},{10,11... | collective-permute-start | bytes 202760 | tf_op jit(solution)/shard_map/ppermute | solution.py:293
  10.7 13.2 %collective-permute-start.6 = (bf16[8,4224]{1,0:T(8,128)(2,1)}, bf16[8,4224]{1,0:T(8,128)(2,1)S(1)}, u32[]{:S(2)}, u32[]{:S(2)}) collective-permute-start(bf16[8,4224]{1,0:T(8,128)(2,1)} %get-tuple-element.32), channel_id=1, source_target_pairs={{0,2},{1,3},{2,0},{3,1},{4,6},{5,7},{6,4},{7,5},{8,10},{9,11},{10,... | collective-permute-start | bytes 202760 | tf_op jit(solution)/shard_map/ppermute | solution.py:293
  14.1 9.9 %collective-permute-start.7 = (bf16[8,4224]{1,0:T(8,128)(2,1)}, bf16[8,4224]{1,0:T(8,128)(2,1)S(1)}, u32[]{:S(2)}, u32[]{:S(2)}) collective-permute-start(bf16[8,4224]{1,0:T(8,128)(2,1)} %get-tuple-element.32), channel_id=1, source_target_pairs={{0,3},{1,2},{2,1},{3,0},{4,7},{5,6},{6,5},{7,4},{8,11},{9,10},{10,... | collective-permute-start | bytes 202760 | tf_op jit(solution)/shard_map/ppermute | solution.py:293
  14.4 9.5 %copy-start.1 = (bf16[8,4224]{1,0:T(8,128)(2,1)S(1)}, bf16[8,4224]{1,0:T(8,128)(2,1)}, u32[]{:S(2)}) copy-start(bf16[8,4224]{1,0:T(8,128)(2,1)} %get-tuple-element.32) | copy-start | bytes 202756
  15.4 9.3 %collective-permute-start.3 = (bf16[4,8,4224]{2,1,0:T(8,128)(2,1)S(1)}, bf16[4,8,4224]{2,1,0:T(8,128)(2,1)S(1)}, u32[]{:S(2)}, u32[]{:S(2)}) collective-permute-start(bf16[4,8,4224]{2,1,0:T(8,128)(2,1)S(1)} %pad_maximum_fusion.rows_ref), channel_id=1, source_target_pairs={{0,8},{4,12},{8,0},{12,4},{1,9},{5,13},{9,1},{13,5},{2,10},{6,14},... | collective-permute-start | bytes 811016 | tf_op jit(solution)/shard_map/ppermute | solution.py:290
  16.9 2.2 %copy-start = (bf16[1,512,4096]{2,1,0:T(8,128)(2,1)S(1)}, bf16[1,512,4096]{2,1,0:T(8,128)(2,1)}, u32[]{:S(2)}) copy-start(bf16[1,512,4096]{2,1,0:T(8,128)(2,1)} %param.11) | copy-start | bytes 12582916
  24.0 7.8 %collective-permute-start.8 = (bf16[4,8,4224]{2,1,0:T(8,128)(2,1)S(1)}, bf16[4,8,4224]{2,1,0:T(8,128)(2,1)S(1)}, u32[]{:S(2)}, u32[]{:S(2)}) collective-permute-start(bf16[4,8,4224]{2,1,0:T(8,128)(2,1)S(1)} %pad_maximum_fusion.1.rows_ref), channel_id=1, source_target_pairs={{0,8},{4,12},{8,0},{12,4},{1,9},{5,13},{9,1},{13,5},{2,10},{6,14},... | collective-permute-start | bytes 811016 | tf_op jit(solution)/shard_map/ppermute | solution.py:290
  30.4 14.9 %collective-permute-start.9 = (bf16[4,8,16,512]{3,2,1,0:T(8,128)(2,1)S(1)}, bf16[4,8,16,512]{3,2,1,0:T(8,128)(2,1)S(1)}, u32[]{:S(2)}, u32[]{:S(2)}) collective-permute-start(bf16[4,8,16,512]{3,2,1,0:T(8,128)(2,1)S(1)} %score.5), channel_id=1, source_target_pairs={{0,8},{4,12},{8,0},{12,4},{1,9},{5,13},{9,1},{13,5},{2,10},{6,14},... | collective-permute-start | bytes 1572872 | tf_op jit(solution)/shard_map/ppermute | solution.py:290
  36.6 18.2 %collective-permute-start.10 = (bf16[4,8,16,512]{3,2,1,0:T(8,128)(2,1)S(1)}, bf16[4,8,16,512]{3,2,1,0:T(8,128)(2,1)S(1)}, u32[]{:S(2)}, u32[]{:S(2)}) collective-permute-start(bf16[4,8,16,512]{3,2,1,0:T(8,128)(2,1)S(1)} %score.4), channel_id=1, source_target_pairs={{0,8},{4,12},{8,0},{12,4},{1,9},{5,13},{9,1},{13,5},{2,10},{6,14},... | collective-permute-start | bytes 1572872 | tf_op jit(solution)/shard_map/ppermute | solution.py:290
  45.5 9.3 %collective-permute-start.11 = (bf16[8,16,512]{2,1,0:T(8,128)(2,1)S(1)}, bf16[8,16,512]{2,1,0:T(8,128)(2,1)S(1)}, u32[]{:S(2)}, u32[]{:S(2)}) collective-permute-start(bf16[8,16,512]{2,1,0:T(8,128)(2,1)S(1)} %get-tuple-element.53), channel_id=1, source_target_pairs={{0,1},{1,0},{2,3},{3,2},{4,5},{5,4},{6,7},{7,6},{8,9},{9,8},{10,11... | collective-permute-start | bytes 393224 | tf_op jit(solution)/shard_map/ppermute | solution.py:293
  46.4 13.0 %collective-permute-start.15 = (bf16[8,16,512]{2,1,0:T(8,128)(2,1)S(1)}, bf16[8,16,512]{2,1,0:T(8,128)(2,1)S(1)}, u32[]{:S(2)}, u32[]{:S(2)}) collective-permute-start(bf16[8,16,512]{2,1,0:T(8,128)(2,1)S(1)} %get-tuple-element.51), channel_id=1, source_target_pairs={{0,2},{1,3},{2,0},{3,1},{4,6},{5,7},{6,4},{7,5},{8,10},{9,11},{10,... | collective-permute-start | bytes 393224 | tf_op jit(solution)/shard_map/ppermute | solution.py:293
  49.6 9.8 %collective-permute-start.16 = (bf16[8,16,512]{2,1,0:T(8,128)(2,1)S(1)}, bf16[8,16,512]{2,1,0:T(8,128)(2,1)S(1)}, u32[]{:S(2)}, u32[]{:S(2)}) collective-permute-start(bf16[8,16,512]{2,1,0:T(8,128)(2,1)S(1)} %get-tuple-element.50), channel_id=1, source_target_pairs={{0,3},{1,2},{2,1},{3,0},{4,7},{5,6},{6,5},{7,4},{8,11},{9,10},{10,... | collective-permute-start | bytes 393224 | tf_op jit(solution)/shard_map/ppermute | solution.py:293
  55.0 7.3 %collective-permute-start.12 = (bf16[8,16,512]{2,1,0:T(8,128)(2,1)S(1)}, bf16[8,16,512]{2,1,0:T(8,128)(2,1)S(1)}, u32[]{:S(2)}, u32[]{:S(2)}) collective-permute-start(bf16[8,16,512]{2,1,0:T(8,128)(2,1)S(1)} %get-tuple-element.56), channel_id=1, source_target_pairs={{0,1},{1,0},{2,3},{3,2},{4,5},{5,4},{6,7},{7,6},{8,9},{9,8},{10,11... | collective-permute-start | bytes 393224 | tf_op jit(solution)/shard_map/ppermute | solution.py:293
  55.3 11.3 %collective-permute-start.13 = (bf16[8,16,512]{2,1,0:T(8,128)(2,1)S(1)}, bf16[8,16,512]{2,1,0:T(8,128)(2,1)S(1)}, u32[]{:S(2)}, u32[]{:S(2)}) collective-permute-start(bf16[8,16,512]{2,1,0:T(8,128)(2,1)S(1)} %get-tuple-element.55), channel_id=1, source_target_pairs={{0,2},{1,3},{2,0},{3,1},{4,6},{5,7},{6,4},{7,5},{8,10},{9,11},{10,... | collective-permute-start | bytes 393224 | tf_op jit(solution)/shard_map/ppermute | solution.py:293
  59.1 7.4 %collective-permute-start.14 = (bf16[8,16,512]{2,1,0:T(8,128)(2,1)S(1)}, bf16[8,16,512]{2,1,0:T(8,128)(2,1)S(1)}, u32[]{:S(2)}, u32[]{:S(2)}) collective-permute-start(bf16[8,16,512]{2,1,0:T(8,128)(2,1)S(1)} %get-tuple-element.54), channel_id=1, source_target_pairs={{0,3},{1,2},{2,1},{3,0},{4,7},{5,6},{6,5},{7,4},{8,11},{9,10},{10,... | collective-permute-start | bytes 393224 | tf_op jit(solution)/shard_map/ppermute | solution.py:293
where the time goes:
time: 68.6 us; the launch traced here: 68.3 us
  Pallas kernels  29.9 us (44%)
  starting transfers between devices  21 us (31%)
  waiting for transfers between devices  12.7 us (19%)
  local copies, waits for them, and re-layouts  2.27 us (3%)
  other arithmetic  1.63 us (2%)
  between operations  0.8 us (1%)
    pallas_call x4, Pallas kernels, score(): pl.pallas_call(score_kernel, out_shape=jax.ShapeDtypeStruct((pieces, coun...  20 us
    ppermute x12, starting transfers between devices, along_z(): return lax.ppermute(value, 'proj', [(i, i ^ by) for i in range(places)])  17.6 us
    ppermute x12, waiting for transfers between devices, along_z(): return lax.ppermute(value, 'proj', [(i, i ^ by) for i in range(places)])  8.28 us
    pallas_call x1, Pallas kernels, turn(): pl.pallas_call(turn_kernel, grid=(width // TURN,), out_shape=[turned, tur...  4.78 us
    ppermute x4, waiting for transfers between devices, along_x(): return lax.ppermute(value, 'cls', [(i, i ^ 2 * by) for i in range(owners)])  4.43 us
    pallas_call x2, Pallas kernels, weigh(): pl.pallas_call(functools.partial(weigh_kernel, places, first), grid=(coun...  3.49 us
    ppermute x4, starting transfers between devices, along_x(): return lax.ppermute(value, 'cls', [(i, i ^ 2 * by) for i in range(owners)])  2.9 us
    unnamed x4, local copies, waits for them, and re-layouts  2.19 us
  transfers between devices with their start and end apart: 17, of which 6 were waited for; matrix products, arithmetic and copies ran while one was open for 2% of the time, Pallas kernels for 41%

commit v1 on v0

--- a/solution.py
+++ b/solution.py
@@ -75,32 +75,42 @@
     )(particles, classes.T, windows.T, pose_lists.T, inverse_noise[None, :])
 
 
-def turn_kernel(own_ref, other_ref, own_out, other_out, cos_ref, sin_ref):
-    own_out[...] = own_ref[...].T
-    other_out[...] = other_ref[...].T
-
-    @pl.when(pl.program_id(0) == 0)
-    def _():
-        shift = lax.broadcasted_iota(jnp.int32, cos_ref.shape, 0)
-        c = lax.broadcasted_iota(jnp.int32, cos_ref.shape, 1)
-        kx, ky = c % IMG - IMG // 2, c // IMG
-        turn = (shift % SW - SW // 2) * kx + (shift // SW - SW // 2) * ky
-        cos_ref[...], sin_ref[...] = unit_circle(turn.astype(jnp.float32))
+def turn_kernel(own_any, other_any, own_out, other_out, cos_ref, sin_ref, blocks, sems):
+    _, steps, _, width = blocks.shape
+    loads = [
+        pltpu.make_async_copy(panel.at[:, pl.ds(i * width, width)], blocks.at[n, i], sems.at[n, i])
+        for n, panel in enumerate((own_any, other_any))
+        for i in range(steps)
+    ]
+    for copy in loads:
+        copy.start()
+    shift = lax.broadcasted_iota(jnp.int32, cos_ref.shape, 0)
+    c = lax.broadcasted_iota(jnp.int32, cos_ref.shape, 1)
+    kx, ky = c % IMG - IMG // 2, c // IMG
+    turn = (shift % SW - SW // 2) * kx + (shift // SW - SW // 2) * ky
+    cos_ref[...], sin_ref[...] = unit_circle(turn.astype(jnp.float32))
+    for n, out_ref in enumerate((own_out, other_out)):
+        for i in range(steps):
+            loads[n * steps + i].wait()
+            out_ref[i * width:(i + 1) * width, :] = blocks[n, i].T
 
 
 def turn(own_panel, other_panel):
     depth, width = own_panel.shape
     turned = jax.ShapeDtypeStruct((width, depth), own_panel.dtype)
     table = jax.ShapeDtypeStruct((SH, KF), jnp.float32)
-    fixed = pl.BlockSpec((SH, KF), lambda i: (0, 0))
+    steps = width // TURN
     return pl.pallas_call(
         turn_kernel,
-        grid=(width // TURN,),
         out_shape=[turned, turned, table, table],
-        in_specs=[pl.BlockSpec((depth, TURN), lambda i: (0, i))] * 2,
-        out_specs=[pl.BlockSpec((TURN, depth), lambda i: (i, 0))] * 2 + [fixed] * 2,
+        in_specs=[pl.BlockSpec(memory_space=pl.ANY)] * 2,
+        out_specs=[pl.BlockSpec(memory_space=pltpu.VMEM)] * 4,
+        scratch_shapes=[
+            pltpu.VMEM((2, steps, depth, TURN), jnp.bfloat16),
+            pltpu.SemaphoreType.DMA((2, steps)),
+        ],
         compiler_params=pltpu.CompilerParams(vmem_limit_bytes=20 * 1024 * 1024),
-        cost_estimate=pl.CostEstimate(flops=0, bytes_accessed=16 << 20, transcendentals=0),
+        cost_estimate=pl.CostEstimate(flops=1 << 32, bytes_accessed=0, transcendentals=0),
         name="turn",
     )(own_panel, other_panel)
 

time: 68.6 us -> 67.6 us (0.985)
  Pallas kernels: 29.9 us -> 24.4 us
  starting transfers between devices: 21 us -> 25.9 us
  waiting for transfers between devices: 12.7 us -> 11.8 us
    ppermute x4, starting transfers between devices: 2.9 us -> 7.79 us  [along_x(): return lax.ppermute(value, 'cls', [(i, i ^ 2 * by) for i in range(owners)])]
    pallas_call x4, Pallas kernels: 20 us -> 15.6 us  [score(): pl.pallas_call(score_kernel, out_shape=jax.ShapeDtypeStruct((pieces, coun...]
    ppermute x4, waiting for transfers between devices: 4.43 us -> 2.81 us  [along_x(): return lax.ppermute(value, 'cls', [(i, i ^ 2 * by) for i in range(owners)])]
    pallas_call x1, Pallas kernels: 4.78 us -> 3.69 us  [turn(): pl.pallas_call(turn_kernel, out_shape=[turned, turned, table, table], in_...]
  transfers between devices with their start and end apart: 17 -> 17, of which waited for: 6 -> 6; matrix products, arithmetic and copies ran while one was open for 2% -> 3% of each run, Pallas kernels for 41% -> 34%
where the time goes in v1:
time: 67.6 us; the launch traced here: 66.8 us
  starting transfers between devices  25.9 us (38%)
  Pallas kernels  24.4 us (36%)
  waiting for transfers between devices  11.8 us (17%)
  local copies, waits for them, and re-layouts  2.27 us (3%)
  other arithmetic  1.63 us (2%)
  between operations  0.78 us (1%)
    ppermute x12, starting transfers between devices, along_z(): return lax.ppermute(value, 'proj', [(i, i ^ by) for i in range(places)])  17.6 us
    pallas_call x4, Pallas kernels, score(): pl.pallas_call(score_kernel, out_shape=jax.ShapeDtypeStruct((pieces, coun...  15.6 us
    ppermute x12, waiting for transfers between devices, along_z(): return lax.ppermute(value, 'proj', [(i, i ^ by) for i in range(places)])  8.94 us
    ppermute x4, starting transfers between devices, along_x(): return lax.ppermute(value, 'cls', [(i, i ^ 2 * by) for i in range(owners)])  7.79 us
    pallas_call x1, Pallas kernels, turn(): pl.pallas_call(turn_kernel, out_shape=[turned, turned, table, table], in_...  3.69 us
    pallas_call x2, Pallas kernels, weigh(): pl.pallas_call(functools.partial(weigh_kernel, places, first), grid=(coun...  3.49 us
    ppermute x4, waiting for transfers between devices, along_x(): return lax.ppermute(value, 'cls', [(i, i ^ 2 * by) for i in range(owners)])  2.81 us
    unnamed x4, local copies, waits for them, and re-layouts  2.19 us
  transfers between devices with their start and end apart: 17, of which 6 were waited for; matrix products, arithmetic and copies ran while one was open for 3% of the time, Pallas kernels for 34%

profile of v1, /device:TPU:0, one launch (start us, length us, event | category | flops | bytes accessed | tf_op | source)
XLA Modules:
  0.0 66.8 jit_solution(5192865512484838812)
XLA Ops:
  0.6 0.5 collective-permute-start.4
  1.1 1.7 %pack.1 = (bf16[8,4224]{1,0:T(8,128)(2,1)}, bf16[8,4224]{1,0:T(8,128)(2,1)}) custom-call(bf16[16,4096]{1,0:T(8,128)(2,1)} %particles_ref.1, s32[1,16]{1,0:T(1,128)} %bitcast.45, s32[2,16]{1,0:T(2,128)} %bitcast.44, s32[8,16]{1,0:T(8,128)} %bitcast.43, bf16[1,16]{1,0:T(2,128)(2,1)} %bitcast.46), custom_call_target="tpu_custom_call" | custom-call | tf_op jit(solution)/shard_map/pack/pallas_call | solution.py:68
  2.8 4.6 %collective-permute-start.2 = (bf16[8,4224]{1,0:T(8,128)(2,1)}, bf16[8,4224]{1,0:T(8,128)(2,1)S(1)}, u32[]{:S(2)}, u32[]{:S(2)}) collective-permute-start(bf16[8,4224]{1,0:T(8,128)(2,1)} %get-tuple-element.26), channel_id=1, source_target_pairs={{0,3},{1,2},{2,1},{3,0},{4,7},{5,6},{6,5},{7,4},{8,11},{9,10},{10,... | collective-permute-start | bytes 202760 | tf_op jit(solution)/shard_map/ppermute | solution.py:303
  7.4 0.0 collective-permute-start
  7.4 0.6 collective-permute-start.1
  8.0 1.5 %collective-permute-start.5 = (bf16[8,4224]{1,0:T(8,128)(2,1)}, bf16[8,4224]{1,0:T(8,128)(2,1)S(1)}, u32[]{:S(2)}, u32[]{:S(2)}) collective-permute-start(bf16[8,4224]{1,0:T(8,128)(2,1)} %get-tuple-element.32), channel_id=1, source_target_pairs={{0,1},{1,0},{2,3},{3,2},{4,5},{5,4},{6,7},{7,6},{8,9},{9,8},{10,11... | collective-permute-start | bytes 202760 | tf_op jit(solution)/shard_map/ppermute | solution.py:303
  9.5 1.2 %collective-permute-done.2 = bf16[8,4224]{1,0:T(8,128)(2,1)S(1)} collective-permute-done((bf16[8,4224]{1,0:T(8,128)(2,1)}, bf16[8,4224]{1,0:T(8,128)(2,1)S(1)}, u32[]{:S(2)}, u32[]{:S(2)}) %collective-permute-start.2) | collective-permute-done | bytes 67616 | tf_op jit(solution)/shard_map/ppermute | solution.py:303
  10.7 1.7 %collective-permute-start.6 = (bf16[8,4224]{1,0:T(8,128)(2,1)}, bf16[8,4224]{1,0:T(8,128)(2,1)S(1)}, u32[]{:S(2)}, u32[]{:S(2)}) collective-permute-start(bf16[8,4224]{1,0:T(8,128)(2,1)} %get-tuple-element.32), channel_id=1, source_target_pairs={{0,2},{1,3},{2,0},{3,1},{4,6},{5,7},{6,4},{7,5},{8,10},{9,11},{10,... | collective-permute-start | bytes 202760 | tf_op jit(solution)/shard_map/ppermute | solution.py:303
  12.4 1.7 %collective-permute-done = bf16[8,4224]{1,0:T(8,128)(2,1)S(1)} collective-permute-done((bf16[8,4224]{1,0:T(8,128)(2,1)}, bf16[8,4224]{1,0:T(8,128)(2,1)S(1)}, u32[]{:S(2)}, u32[]{:S(2)}) %collective-permute-start) | collective-permute-done | bytes 67616 | tf_op jit(solution)/shard_map/ppermute | solution.py:303
  14.1 0.3 collective-permute-start.7
  14.4 0.0 collective-permute-done.1
  14.4 1.0 %pad_maximum_fusion.rows_ref = bf16[4,8,4224]{2,1,0:T(8,128)(2,1)S(1)} fusion(bf16[1,8,4224]{2,1,0:T(8,128)(2,1)S(1)} %bitcast.38, bf16[1,8,4224]{2,1,0:T(8,128)(2,1)S(1)} %bitcast.40, bf16[1,8,4224]{2,1,0:T(8,128)(2,1)S(1)} %bitcast.39, bf16[1,8,4224]{2,1,0:T(8,128)(2,1)} %bitcast.37), kind=kLoop, calls=%fused_computation.2 | loop fusion | flops 405504 | bytes 540672 | tf_op jit(solution)/shard_map/stack | solution.py:310
  15.4 1.6 %collective-permute-start.3 = (bf16[4,8,4224]{2,1,0:T(8,128)(2,1)S(1)}, bf16[4,8,4224]{2,1,0:T(8,128)(2,1)S(1)}, u32[]{:S(2)}, u32[]{:S(2)}) collective-permute-start(bf16[4,8,4224]{2,1,0:T(8,128)(2,1)S(1)} %pad_maximum_fusion.rows_ref), channel_id=1, source_target_pairs={{0,8},{4,12},{8,0},{12,4},{1,9},{5,13},{9,1},{13,5},{2,10},{6,14},... | collective-permute-start | bytes 811016 | tf_op jit(solution)/shard_map/ppermute | solution.py:300
  16.9 0.0 collective-permute-done.4.other_any
  16.9 2.2 %copy-done = bf16[1,512,4096]{2,1,0:T(8,128)(2,1)S(1)} copy-done((bf16[1,512,4096]{2,1,0:T(8,128)(2,1)S(1)}, bf16[1,512,4096]{2,1,0:T(8,128)(2,1)}, u32[]{:S(2)}) %copy-start) | copy-done | bytes 4194328
  19.1 3.7 %turn.1 = (bf16[4096,512]{1,0:T(8,128)(2,1)S(1)}, bf16[4096,512]{1,0:T(8,128)(2,1)S(1)}, f32[16,2048]{1,0:T(8,128)S(1)}, f32[16,2048]{1,0:T(8,128)S(1)}) custom-call(bf16[512,4096]{1,0:T(8,128)(2,1)S(1)} %bitcast.34, bf16[512,4096]{1,0:T(8,128)(2,1)} %collective-permute-done.4.other_any), custom_call_target="tpu_custom_call" | custom-call | flops 4294967296 | tf_op jit(solution)/shard_map/turn/pallas_call | solution.py:103
  22.8 0.0 collective-permute-done.5
  22.8 0.0 collective-permute-done.6
  22.8 0.0 collective-permute-done.7
  22.9 0.6 collective-permute-start.8
  23.5 0.1 pad_add_fusion.me_ref
  23.6 0.0 collective-permute-done.3.rows_ref
  23.6 3.7 %score.5 = bf16[4,8,16,512]{3,2,1,0:T(8,128)(2,1)S(1)} custom-call(s32[3]{0:T(128)S(1)} %pad_add_fusion.me_ref, bf16[4,8,4224]{2,1,0:T(8,128)(2,1)S(1)} %collective-permute-done.3.rows_ref, bf16[4096,512]{1,0:T(8,128)(2,1)S(1)} %get-tuple-element.37.own_any, bf16[4096,512]{1,0:T(8,128)(2,1)S(1)} %get-tuple-element.38.other_any, ...), custom_call_target="tpu_custom_call" | custom-call | flops 2147483648 | bytes 16777216 | tf_op jit(solution)/shard_map/score/pallas_call | solution.py:215
  27.3 3.5 %collective-permute-start.9 = (bf16[4,8,16,512]{3,2,1,0:T(8,128)(2,1)S(1)}, bf16[4,8,16,512]{3,2,1,0:T(8,128)(2,1)S(1)}, u32[]{:S(2)}, u32[]{:S(2)}) collective-permute-start(bf16[4,8,16,512]{3,2,1,0:T(8,128)(2,1)S(1)} %score.5), channel_id=1, source_target_pairs={{0,8},{4,12},{8,0},{12,4},{1,9},{5,13},{9,1},{13,5},{2,10},{6,14},... | collective-permute-start | bytes 1572872 | tf_op jit(solution)/shard_map/ppermute | solution.py:300
  30.8 0.0 collective-permute-done.8.rows_ref
  30.8 3.7 %score.4 = bf16[4,8,16,512]{3,2,1,0:T(8,128)(2,1)S(1)} custom-call(s32[3]{0:T(128)S(1)} %pad_add_fusion.me_ref, bf16[4,8,4224]{2,1,0:T(8,128)(2,1)S(1)} %collective-permute-done.8.rows_ref, bf16[4096,512]{1,0:T(8,128)(2,1)S(1)} %get-tuple-element.37.own_any, bf16[4096,512]{1,0:T(8,128)(2,1)S(1)} %get-tuple-element.38.other_any, ...), custom_call_target="tpu_custom_call" | custom-call | flops 2147483648 | bytes 16777216 | tf_op jit(solution)/shard_map/score/pallas_call | solution.py:215
  34.5 2.1 %collective-permute-start.10 = (bf16[4,8,16,512]{3,2,1,0:T(8,128)(2,1)S(1)}, bf16[4,8,16,512]{3,2,1,0:T(8,128)(2,1)S(1)}, u32[]{:S(2)}, u32[]{:S(2)}) collective-permute-start(bf16[4,8,16,512]{3,2,1,0:T(8,128)(2,1)S(1)} %score.4), channel_id=1, source_target_pairs={{0,8},{4,12},{8,0},{12,4},{1,9},{5,13},{9,1},{13,5},{2,10},{6,14},... | collective-permute-start | bytes 1572872 | tf_op jit(solution)/shard_map/ppermute | solution.py:300
  36.6 0.1 convert_reduce_fusion.1
  36.8 4.6 %score.6 = bf16[4,8,16,512]{3,2,1,0:T(8,128)(2,1)S(1)} custom-call(s32[3]{0:T(128)S(1)} %pad_add_fusion.me_ref, bf16[4,8,4224]{2,1,0:T(8,128)(2,1)S(1)} %pad_maximum_fusion.rows_ref, bf16[4096,512]{1,0:T(8,128)(2,1)S(1)} %get-tuple-element.37.own_any, bf16[4096,512]{1,0:T(8,128)(2,1)S(1)} %get-tuple-element.38.other_any, ...), custom_call_target="tpu_custom_call" | custom-call | flops 2147483648 | bytes 16777216 | tf_op jit(solution)/shard_map/score/pallas_call | solution.py:215
  41.4 2.3 %collective-permute-done.9 = bf16[4,8,16,512]{3,2,1,0:T(8,128)(2,1)S(1)} collective-permute-done((bf16[4,8,16,512]{3,2,1,0:T(8,128)(2,1)S(1)}, bf16[4,8,16,512]{3,2,1,0:T(8,128)(2,1)S(1)}, u32[]{:S(2)}, u32[]{:S(2)}) %collective-permute-start.9) | collective-permute-done | bytes 524320 | tf_op jit(solution)/shard_map/ppermute | solution.py:300
  43.7 0.1 broadcast_select_fusion.1
  43.8 0.9 %collective-permute-start.11 = (bf16[8,16,512]{2,1,0:T(8,128)(2,1)S(1)}, bf16[8,16,512]{2,1,0:T(8,128)(2,1)S(1)}, u32[]{:S(2)}, u32[]{:S(2)}) collective-permute-start(bf16[8,16,512]{2,1,0:T(8,128)(2,1)S(1)} %get-tuple-element.53), channel_id=1, source_target_pairs={{0,1},{1,0},{2,3},{3,2},{4,5},{5,4},{6,7},{7,6},{8,9},{9,8},{10,11... | collective-permute-start | bytes 393224 | tf_op jit(solution)/shard_map/ppermute | solution.py:303
  44.8 3.3 %collective-permute-start.15 = (bf16[8,16,512]{2,1,0:T(8,128)(2,1)S(1)}, bf16[8,16,512]{2,1,0:T(8,128)(2,1)S(1)}, u32[]{:S(2)}, u32[]{:S(2)}) collective-permute-start(bf16[8,16,512]{2,1,0:T(8,128)(2,1)S(1)} %get-tuple-element.51), channel_id=1, source_target_pairs={{0,2},{1,3},{2,0},{3,1},{4,6},{5,7},{6,4},{7,5},{8,10},{9,11},{10,... | collective-permute-start | bytes 393224 | tf_op jit(solution)/shard_map/ppermute | solution.py:303
  48.0 0.2 collective-permute-start.16
  48.3 0.1 convert_reduce_fusion
  48.4 3.6 %score.7 = bf16[4,8,16,512]{3,2,1,0:T(8,128)(2,1)S(1)} custom-call(s32[3]{0:T(128)S(1)} %pad_add_fusion.me_ref, bf16[4,8,4224]{2,1,0:T(8,128)(2,1)S(1)} %pad_maximum_fusion.1.rows_ref, bf16[4096,512]{1,0:T(8,128)(2,1)S(1)} %get-tuple-element.37.own_any, bf16[4096,512]{1,0:T(8,128)(2,1)S(1)} %get-tuple-element.38.other_any, ...), custom_call_target="tpu_custom_call" | custom-call | flops 2147483648 | bytes 16777216 | tf_op jit(solution)/shard_map/score/pallas_call | solution.py:215
  52.1 0.0 collective-permute-done.11.refs_1_
  52.1 0.5 collective-permute-done.10
  52.6 0.1 broadcast_select_fusion
  52.8 0.6 collective-permute-start.12
  53.4 3.1 %collective-permute-start.13 = (bf16[8,16,512]{2,1,0:T(8,128)(2,1)S(1)}, bf16[8,16,512]{2,1,0:T(8,128)(2,1)S(1)}, u32[]{:S(2)}, u32[]{:S(2)}) collective-permute-start(bf16[8,16,512]{2,1,0:T(8,128)(2,1)S(1)} %get-tuple-element.55), channel_id=1, source_target_pairs={{0,2},{1,3},{2,0},{3,1},{4,6},{5,7},{6,4},{7,5},{8,10},{9,11},{10,... | collective-permute-start | bytes 393224 | tf_op jit(solution)/shard_map/ppermute | solution.py:303
  56.5 0.7 %collective-permute-start.14 = (bf16[8,16,512]{2,1,0:T(8,128)(2,1)S(1)}, bf16[8,16,512]{2,1,0:T(8,128)(2,1)S(1)}, u32[]{:S(2)}, u32[]{:S(2)}) collective-permute-start(bf16[8,16,512]{2,1,0:T(8,128)(2,1)S(1)} %get-tuple-element.54), channel_id=1, source_target_pairs={{0,3},{1,2},{2,1},{3,0},{4,7},{5,6},{6,5},{7,4},{8,11},{9,10},{10,... | collective-permute-start | bytes 393224 | tf_op jit(solution)/shard_map/ppermute | solution.py:303
  57.2 0.0 collective-permute-done.15.refs_2_
  57.2 1.8 %weigh.2 = (f32[16,16,2048]{2,1,0:T(8,128)}, f32[1,16]{1,0:T(1,128)S(1)}) custom-call(s32[3]{0:T(128)S(1)} %pad_add_fusion.me_ref, bf16[8,16,512]{2,1,0:T(8,128)(2,1)S(1)} %get-tuple-element.52.refs_0_, bf16[8,16,512]{2,1,0:T(8,128)(2,1)S(1)} %collective-permute-done.11.refs_1_, bf16[8,16,512]{2,1,0:T(8,128)(2,1)S(1)} %collective-permute-done.15.refs_2_, ...), custom_call_target="tpu_custom_call" | custom-call | tf_op jit(solution)/shard_map/weigh/pallas_call | solution.py:273
  59.0 2.0 %collective-permute-done.12.refs_1_ = bf16[8,16,512]{2,1,0:T(8,128)(2,1)S(1)} collective-permute-done((bf16[8,16,512]{2,1,0:T(8,128)(2,1)S(1)}, bf16[8,16,512]{2,1,0:T(8,128)(2,1)S(1)}, u32[]{:S(2)}, u32[]{:S(2)}) %collective-permute-start.12) | collective-permute-done | bytes 131104 | tf_op jit(solution)/shard_map/ppermute | solution.py:303
  61.0 4.1 %collective-permute-done.13.refs_2_ = bf16[8,16,512]{2,1,0:T(8,128)(2,1)S(1)} collective-permute-done((bf16[8,16,512]{2,1,0:T(8,128)(2,1)S(1)}, bf16[8,16,512]{2,1,0:T(8,128)(2,1)S(1)}, u32[]{:S(2)}, u32[]{:S(2)}) %collective-permute-start.13) | collective-permute-done | bytes 131104 | tf_op jit(solution)/shard_map/ppermute | solution.py:303
  65.0 0.0 collective-permute-done.14.refs_3_
  65.0 1.7 %weigh.3 = (f32[16,16,2048]{2,1,0:T(8,128)}, f32[1,16]{1,0:T(1,128)}) custom-call(s32[3]{0:T(128)S(1)} %pad_add_fusion.me_ref, bf16[8,16,512]{2,1,0:T(8,128)(2,1)S(1)} %get-tuple-element.57.refs_0_, bf16[8,16,512]{2,1,0:T(8,128)(2,1)S(1)} %collective-permute-done.12.refs_1_, ...), custom_call_target="tpu_custom_call", output_to_operand_aliasing={{0}: (5, {})} | custom-call | tf_op jit(solution)/shard_map/weigh/pallas_call | solution.py:273
  (9 shorter events, 0.2 us)
Async XLA Ops:
  0.6 16.3 %collective-permute-start.4 = (bf16[512,4096]{1,0:T(8,128)(2,1)}, bf16[512,4096]{1,0:T(8,128)(2,1)}, u32[]{:S(2)}, u32[]{:S(2)}) collective-permute-start(bf16[512,4096]{1,0:T(8,128)(2,1)} %bitcast.33), channel_id=1, source_target_pairs={{0,4},{4,0},{8,12},{12,8},{1,5},{5,1},{9,13},{13,9},{2,6},{6,2},{1... | collective-permute-start | bytes 12582920 | tf_op jit(solution)/shard_map/ppermute | solution.py:307
  2.8 7.9 %collective-permute-start.2 = (bf16[8,4224]{1,0:T(8,128)(2,1)}, bf16[8,4224]{1,0:T(8,128)(2,1)S(1)}, u32[]{:S(2)}, u32[]{:S(2)}) collective-permute-start(bf16[8,4224]{1,0:T(8,128)(2,1)} %get-tuple-element.26), channel_id=1, source_target_pairs={{0,3},{1,2},{2,1},{3,0},{4,7},{5,6},{6,5},{7,4},{8,11},{9,10},{10,... | collective-permute-start | bytes 202760 | tf_op jit(solution)/shard_map/ppermute | solution.py:303
  7.4 6.6 %collective-permute-start = (bf16[8,4224]{1,0:T(8,128)(2,1)}, bf16[8,4224]{1,0:T(8,128)(2,1)S(1)}, u32[]{:S(2)}, u32[]{:S(2)}) collective-permute-start(bf16[8,4224]{1,0:T(8,128)(2,1)} %get-tuple-element.26), channel_id=1, source_target_pairs={{0,1},{1,0},{2,3},{3,2},{4,5},{5,4},{6,7},{7,6},{8,9},{9,8},{10,11... | collective-permute-start | bytes 202760 | tf_op jit(solution)/shard_map/ppermute | solution.py:303
  7.4 7.0 %collective-permute-start.1 = (bf16[8,4224]{1,0:T(8,128)(2,1)}, bf16[8,4224]{1,0:T(8,128)(2,1)S(1)}, u32[]{:S(2)}, u32[]{:S(2)}) collective-permute-start(bf16[8,4224]{1,0:T(8,128)(2,1)} %get-tuple-element.26), channel_id=1, source_target_pairs={{0,2},{1,3},{2,0},{3,1},{4,6},{5,7},{6,4},{7,5},{8,10},{9,11},{10,... | collective-permute-start | bytes 202760 | tf_op jit(solution)/shard_map/ppermute | solution.py:303
  8.0 14.8 %collective-permute-start.5 = (bf16[8,4224]{1,0:T(8,128)(2,1)}, bf16[8,4224]{1,0:T(8,128)(2,1)S(1)}, u32[]{:S(2)}, u32[]{:S(2)}) collective-permute-start(bf16[8,4224]{1,0:T(8,128)(2,1)} %get-tuple-element.32), channel_id=1, source_target_pairs={{0,1},{1,0},{2,3},{3,2},{4,5},{5,4},{6,7},{7,6},{8,9},{9,8},{10,11... | collective-permute-start | bytes 202760 | tf_op jit(solution)/shard_map/ppermute | solution.py:303
  10.7 12.1 %collective-permute-start.6 = (bf16[8,4224]{1,0:T(8,128)(2,1)}, bf16[8,4224]{1,0:T(8,128)(2,1)S(1)}, u32[]{:S(2)}, u32[]{:S(2)}) collective-permute-start(bf16[8,4224]{1,0:T(8,128)(2,1)} %get-tuple-element.32), channel_id=1, source_target_pairs={{0,2},{1,3},{2,0},{3,1},{4,6},{5,7},{6,4},{7,5},{8,10},{9,11},{10,... | collective-permute-start | bytes 202760 | tf_op jit(solution)/shard_map/ppermute | solution.py:303
  14.1 8.8 %collective-permute-start.7 = (bf16[8,4224]{1,0:T(8,128)(2,1)}, bf16[8,4224]{1,0:T(8,128)(2,1)S(1)}, u32[]{:S(2)}, u32[]{:S(2)}) collective-permute-start(bf16[8,4224]{1,0:T(8,128)(2,1)} %get-tuple-element.32), channel_id=1, source_target_pairs={{0,3},{1,2},{2,1},{3,0},{4,7},{5,6},{6,5},{7,4},{8,11},{9,10},{10,... | collective-permute-start | bytes 202760 | tf_op jit(solution)/shard_map/ppermute | solution.py:303
  14.4 8.4 %copy-start.1 = (bf16[8,4224]{1,0:T(8,128)(2,1)S(1)}, bf16[8,4224]{1,0:T(8,128)(2,1)}, u32[]{:S(2)}) copy-start(bf16[8,4224]{1,0:T(8,128)(2,1)} %get-tuple-element.32) | copy-start | bytes 202756
  15.4 8.2 %collective-permute-start.3 = (bf16[4,8,4224]{2,1,0:T(8,128)(2,1)S(1)}, bf16[4,8,4224]{2,1,0:T(8,128)(2,1)S(1)}, u32[]{:S(2)}, u32[]{:S(2)}) collective-permute-start(bf16[4,8,4224]{2,1,0:T(8,128)(2,1)S(1)} %pad_maximum_fusion.rows_ref), channel_id=1, source_target_pairs={{0,8},{4,12},{8,0},{12,4},{1,9},{5,13},{9,1},{13,5},{2,10},{6,14},... | collective-permute-start | bytes 811016 | tf_op jit(solution)/shard_map/ppermute | solution.py:300
  16.9 2.2 %copy-start = (bf16[1,512,4096]{2,1,0:T(8,128)(2,1)S(1)}, bf16[1,512,4096]{2,1,0:T(8,128)(2,1)}, u32[]{:S(2)}) copy-start(bf16[1,512,4096]{2,1,0:T(8,128)(2,1)} %param.11) | copy-start | bytes 12582916
  22.9 7.9 %collective-permute-start.8 = (bf16[4,8,4224]{2,1,0:T(8,128)(2,1)S(1)}, bf16[4,8,4224]{2,1,0:T(8,128)(2,1)S(1)}, u32[]{:S(2)}, u32[]{:S(2)}) collective-permute-start(bf16[4,8,4224]{2,1,0:T(8,128)(2,1)S(1)} %pad_maximum_fusion.1.rows_ref), channel_id=1, source_target_pairs={{0,8},{4,12},{8,0},{12,4},{1,9},{5,13},{9,1},{13,5},{2,10},{6,14},... | collective-permute-start | bytes 811016 | tf_op jit(solution)/shard_map/ppermute | solution.py:300
  27.3 16.3 %collective-permute-start.9 = (bf16[4,8,16,512]{3,2,1,0:T(8,128)(2,1)S(1)}, bf16[4,8,16,512]{3,2,1,0:T(8,128)(2,1)S(1)}, u32[]{:S(2)}, u32[]{:S(2)}) collective-permute-start(bf16[4,8,16,512]{3,2,1,0:T(8,128)(2,1)S(1)} %score.5), channel_id=1, source_target_pairs={{0,8},{4,12},{8,0},{12,4},{1,9},{5,13},{9,1},{13,5},{2,10},{6,14},... | collective-permute-start | bytes 1572872 | tf_op jit(solution)/shard_map/ppermute | solution.py:300
  34.5 18.1 %collective-permute-start.10 = (bf16[4,8,16,512]{3,2,1,0:T(8,128)(2,1)S(1)}, bf16[4,8,16,512]{3,2,1,0:T(8,128)(2,1)S(1)}, u32[]{:S(2)}, u32[]{:S(2)}) collective-permute-start(bf16[4,8,16,512]{3,2,1,0:T(8,128)(2,1)S(1)} %score.4), channel_id=1, source_target_pairs={{0,8},{4,12},{8,0},{12,4},{1,9},{5,13},{9,1},{13,5},{2,10},{6,14},... | collective-permute-start | bytes 1572872 | tf_op jit(solution)/shard_map/ppermute | solution.py:300
  43.8 8.3 %collective-permute-start.11 = (bf16[8,16,512]{2,1,0:T(8,128)(2,1)S(1)}, bf16[8,16,512]{2,1,0:T(8,128)(2,1)S(1)}, u32[]{:S(2)}, u32[]{:S(2)}) collective-permute-start(bf16[8,16,512]{2,1,0:T(8,128)(2,1)S(1)} %get-tuple-element.53), channel_id=1, source_target_pairs={{0,1},{1,0},{2,3},{3,2},{4,5},{5,4},{6,7},{7,6},{8,9},{9,8},{10,11... | collective-permute-start | bytes 393224 | tf_op jit(solution)/shard_map/ppermute | solution.py:303
  44.8 12.5 %collective-permute-start.15 = (bf16[8,16,512]{2,1,0:T(8,128)(2,1)S(1)}, bf16[8,16,512]{2,1,0:T(8,128)(2,1)S(1)}, u32[]{:S(2)}, u32[]{:S(2)}) collective-permute-start(bf16[8,16,512]{2,1,0:T(8,128)(2,1)S(1)} %get-tuple-element.51), channel_id=1, source_target_pairs={{0,2},{1,3},{2,0},{3,1},{4,6},{5,7},{6,4},{7,5},{8,10},{9,11},{10,... | collective-permute-start | bytes 393224 | tf_op jit(solution)/shard_map/ppermute | solution.py:303
  48.0 9.2 %collective-permute-start.16 = (bf16[8,16,512]{2,1,0:T(8,128)(2,1)S(1)}, bf16[8,16,512]{2,1,0:T(8,128)(2,1)S(1)}, u32[]{:S(2)}, u32[]{:S(2)}) collective-permute-start(bf16[8,16,512]{2,1,0:T(8,128)(2,1)S(1)} %get-tuple-element.50), channel_id=1, source_target_pairs={{0,3},{1,2},{2,1},{3,0},{4,7},{5,6},{6,5},{7,4},{8,11},{9,10},{10,... | collective-permute-start | bytes 393224 | tf_op jit(solution)/shard_map/ppermute | solution.py:303
  52.8 8.2 %collective-permute-start.12 = (bf16[8,16,512]{2,1,0:T(8,128)(2,1)S(1)}, bf16[8,16,512]{2,1,0:T(8,128)(2,1)S(1)}, u32[]{:S(2)}, u32[]{:S(2)}) collective-permute-start(bf16[8,16,512]{2,1,0:T(8,128)(2,1)S(1)} %get-tuple-element.56), channel_id=1, source_target_pairs={{0,1},{1,0},{2,3},{3,2},{4,5},{5,4},{6,7},{7,6},{8,9},{9,8},{10,11... | collective-permute-start | bytes 393224 | tf_op jit(solution)/shard_map/ppermute | solution.py:303
  53.4 11.6 %collective-permute-start.13 = (bf16[8,16,512]{2,1,0:T(8,128)(2,1)S(1)}, bf16[8,16,512]{2,1,0:T(8,128)(2,1)S(1)}, u32[]{:S(2)}, u32[]{:S(2)}) collective-permute-start(bf16[8,16,512]{2,1,0:T(8,128)(2,1)S(1)} %get-tuple-element.55), channel_id=1, source_target_pairs={{0,2},{1,3},{2,0},{3,1},{4,6},{5,7},{6,4},{7,5},{8,10},{9,11},{10,... | collective-permute-start | bytes 393224 | tf_op jit(solution)/shard_map/ppermute | solution.py:303
  56.5 8.5 %collective-permute-start.14 = (bf16[8,16,512]{2,1,0:T(8,128)(2,1)S(1)}, bf16[8,16,512]{2,1,0:T(8,128)(2,1)S(1)}, u32[]{:S(2)}, u32[]{:S(2)}) collective-permute-start(bf16[8,16,512]{2,1,0:T(8,128)(2,1)S(1)} %get-tuple-element.54), channel_id=1, source_target_pairs={{0,3},{1,2},{2,1},{3,0},{4,7},{5,6},{6,5},{7,4},{8,11},{9,10},{10,... | collective-permute-start | bytes 393224 | tf_op jit(solution)/shard_map/ppermute | solution.py:303
